TPU v7x, 256 devices: a whole 4x4x8 slice. The times are simulated.
256 devices in a mesh: tok: 64 (over z, x, core), head: 4 (over y).
Axes of the slice: x: 4, y: 4, z: 8, core: 2. Of those that a mesh axis runs over, the one named last changes fastest.
Arguments:
- atom_single: bfloat16 [30720, 128], P('tok'), may hold values from -80 to 80
- atom_bias: bfloat16 [30720, 4, 128], P('tok'), may hold values from -5 to 320
- atom_token: int32 [30720], P('tok'), may hold values from 0 to 3071, as said below
- atom_count: int32 [3072], P('tok'), may hold values from 1 to 19, as said below
- token_single: bfloat16 [3072, 384], P('tok'), may hold values from -80 to 80
- pair: bfloat16 [3072, 128, 3072], P('tok', 'head'), may hold values from -5 to 24
- atom_qkv: bfloat16 [128, 3, 128], replicated, may hold values from -0.5 to 0.5
- atom_wo: bfloat16 [128, 128], replicated, may hold values from -0.5 to 0.5
- atom_agg: bfloat16 [128, 384], replicated, may hold values from -0.5 to 0.5
- token_qkvg: bfloat16 [384, 4, 384], replicated, may hold values from -0.3125 to 0.3125
- pair_weight: bfloat16 [128, 16], P('head'), may hold values from -0.75 to 0.75
- token_wo: bfloat16 [384, 384], P('head'), may hold values from -0.3125 to 0.3125
Outputs:
- atom_out: bfloat16 [30720, 128], P('tok')
- token_out: bfloat16 [3072, 384], P('tok', 'head')
Inputs may be any that keep to these rules, and one draw needn't show every extreme that they name: `atom_count`: the tokens of each aligned block of 192 tokens have 4 * 480 atoms together. `atom_token`: never falls; token t is named atom_count[t] times.
All inputs are finite; a program needn't handle non-finite values.
Results may differ from a plain program's by a relative error of at most 0.006.
Values may be sent and summed in bfloat16 or wider, within the bound.
A program may use at most 128 MiB of HBM per device.

v0:
```python
import functools
import math

import jax
import jax.numpy as jnp
from jax import lax
from jax.experimental import pallas as pl
from jax.experimental.pallas import tpu as pltpu
from jax.sharding import PartitionSpec as P

ATOM_HEADS = 4
WQ = 32
WK = 128
RIM = (WK - WQ) // 2
BLOCK_DEVS = 4
HEAD_SIZE = 24
ATOM_HEAD_SIZE = 32
EPS = 1e-05

Y = 4
CORES = 2
ROWS = 8
CH = 32
HL = 4
CHUNK = HL * ROWS
LANES = 128

PAIR_MID = 9.5
PAIR_HALF = 14.5
CODE_MAX = 32700.0

F32 = jnp.float32
BF16 = jnp.bfloat16
I16 = jnp.int16
MESH = pl.DeviceIdType.MESH

OPP_UP, OPP_DN, DIR_UP, DIR_DN, FWD_UP, FWD_DN = range(6)


def iota(shape, dim):
    return lax.broadcasted_iota(jnp.int32, shape, dim)


def dot(a, b):
    return jnp.dot(a, b, preferred_element_type=F32)


def dot_nt(a, b):
    return lax.dot_general(a, b, (((1,), (1,)), ((), ())), preferred_element_type=F32)


def mask(cond):
    return jnp.where(cond, 1.0, 0.0).astype(F32)


def normalize(rows):
    mean = jnp.mean(rows, axis=-1, keepdims=True)
    centered = rows - mean
    spread = jnp.mean(centered * centered, axis=-1, keepdims=True)
    return centered * lax.rsqrt(spread + EPS)


def fused(
    zs,
    xs,
    atom_single,
    atom_bias,
    atom_token,
    atom_count,
    token_single,
    pair,
    atom_qkv,
    atom_wo,
    atom_agg,
    token_qkvg,
    pair_weight,
    token_wo,
    atom_out,
    token_out,
    single_v,
    bias_v,
    name_v,
    count_v,
    tok_v,
    pair_v,
    aqkv_v,
    awo_v,
    agg_v,
    qkvg_v,
    two_v,
    kv_pad,
    weights,
    own,
    hold_up,
    hold_dn,
    opp_up_s,
    opp_dn_s,
    dir_up_s,
    dir_dn_s,
    fwd_up_s,
    fwd_dn_s,
    opp_up_r,
    opp_dn_r,
    dir_up_r,
    dir_dn_r,
    fwd_up_r,
    fwd_dn_r,
    sum_s,
    sum_r,
    kv_all,
    score,
    mixed,
    fin_s,
    fin_r,
    proj_v,
    out_v,
    in_sem,
    pair_sem,
    halo_s,
    halo_r,
    w_s,
    w_r,
    y_s,
    opp_r,
    dir_r,
    fwd_r,
    sum_ss,
    sum_rs,
    z_s,
    z_r,
    x_s,
    x_r,
    c_s,
    c_r,
    fin_ss,
    fin_rs,
    known,
    near,
):
    tok = lax.axis_index("tok")
    y = lax.axis_index("head")
    devs = zs * xs * CORES
    z = lax.div(tok, xs * CORES)
    x = lax.rem(lax.div(tok, CORES), xs)
    c = lax.rem(tok, CORES)
    place = lax.rem(tok, BLOCK_DEVS)
    groups, depth, keys = pair_v.shape
    half = keys // 2
    here = tok_v.shape[0]
    atoms = single_v.shape[0]
    windows = atoms // WQ
    columns = HL * HEAD_SIZE
    paired = groups // 2

    def tok_of(z_, x_, c_):
        return (z_ * xs + x_) * CORES + c_

    def y_at(k):
        return lax.rem(y + k, Y)

    def x_at(k):
        return lax.rem(x + k, xs)

    def mate(k):
        return tok - place + lax.rem(place + k, BLOCK_DEVS)

    up, dn = {"head": y_at(1)}, {"head": y_at(3)}

    def remote(src, dst, send, recv, device):
        return pltpu.make_async_remote_copy(
            src_ref=src,
            dst_ref=dst,
            send_sem=send,
            recv_sem=recv,
            device_id=device,
            device_id_type=MESH,
        )

    def signal(sem, device):
        pl.semaphore_signal(sem, inc=1, device_id=device, device_id_type=MESH)

    barrier = pltpu.get_barrier_semaphore()
    for k in range(1, Y):
        signal(barrier, {"head": y_at(k)})

    loads = [
        (pair_weight, weights.at[0]),
        (atom_single, single_v),
        (atom_qkv, aqkv_v),
        (atom_bias, bias_v),
        (atom_wo, awo_v),
        (atom_agg, agg_v),
        (atom_token, name_v),
        (atom_count, count_v),
        (token_qkvg, qkvg_v),
        (token_single, tok_v),
        (token_wo, two_v),
    ]
    loads = [pltpu.make_async_copy(a, b, in_sem.at[i]) for i, (a, b) in enumerate(loads)]

    def pair_load(g):
        return pltpu.make_async_copy(
            pair.at[pl.ds(pl.multiple_of(g * depth, depth), depth), :],
            pair_v.at[g],
            pair_sem.at[g],
        )

    head_loads = [
        pltpu.make_async_copy(
            pair.at[pl.ds(0, depth), pl.ds(side * half, half)],
            pair_v.at[0, :, pl.ds(side * half, half)],
            pair_sem.at[side * groups],
        )
        for side in range(2)
    ]
    loads[0].start()
    for load in head_loads:
        load.start()
    loads[1].start()
    loads[2].start()
    for g in range(1, groups):
        pair_load(g).start()
    for load in loads[3:]:
        load.start()

    first_core = c == 0
    edges = []
    for k in range(1, BLOCK_DEVS):
        same = lax.div(place, CORES) == lax.div(lax.rem(place + k, BLOCK_DEVS), CORES)
        edges.append((None, jnp.where(same, first_core, place + k >= BLOCK_DEVS), mate(k)))
    for k in sorted({1, xs - 1}):
        edges.append((None, x + k >= xs, tok_of(z, x_at(k), c)))
    edges.append((None, first_core, tok_of(z, x, 1 - c)))
    edges.append((tok > 0, first_core, tok - 1))
    edges.append((tok < devs - 1, first_core, tok + 1))
    edges.append((z > 0, True, tok - xs * CORES))
    edges.append((z < zs - 1, False, tok + xs * CORES))

    def both(a, b):
        return b if a is None else a if b is True else jnp.logical_and(a, b)

    waited, waiting, expected, back = [], [], Y - 1, 0
    for there, waits, other in edges:
        if waits is not False:
            waited.append((both(there, waits), other))
            expected = expected + waited[-1][0].astype(jnp.int32)
        if waits is not True:
            waiting.append((both(there, True if waits is False else jnp.logical_not(waits)), other))
            back = back + waiting[-1][0].astype(jnp.int32)

    def signal_all(sem, group):
        for there, other in group:

            @pl.when(there)
            def _():
                signal(sem, {"tok": other})

    signal_all(barrier, waiting)

    loads[0].wait()
    wt = weights[0]
    heads = wt.shape[0]
    row = iota((Y * CHUNK, heads), 0)
    owner = lax.rem(y + lax.div(row, CHUNK), Y)
    pick = iota((Y * CHUNK, heads), 1) == owner * HL + lax.rem(lax.div(row, ROWS), HL)
    picked = dot(mask(pick).astype(BF16), wt).astype(BF16)
    spread = mask(iota((CH, depth), 0) == lax.rem(iota((CH, depth), 1), CH)).astype(BF16)
    diag = lax.div(iota((Y * CHUNK, depth), 1), CH) == lax.rem(iota((Y * CHUNK, depth), 0), ROWS)
    lhs = (dot(picked, spread) * mask(diag)).astype(BF16)
    picked_f = picked.astype(F32)
    mid = PAIR_MID * jnp.sum(picked_f, axis=1, keepdims=True)
    reach = jnp.maximum(PAIR_HALF * jnp.sum(jnp.abs(picked_f), axis=1, keepdims=True), 1e-20)
    inv = CODE_MAX / reach

    buffers = {
        OPP_UP: (opp_up_s, opp_up_r, up),
        OPP_DN: (opp_dn_s, opp_dn_r, dn),
        DIR_UP: (dir_up_s, dir_up_r, up),
        DIR_DN: (dir_dn_s, dir_dn_r, dn),
        FWD_UP: (fwd_up_s, fwd_up_r, up),
        FWD_DN: (fwd_dn_s, fwd_dn_r, dn),
    }

    def landed(kind, g):
        if kind in (OPP_UP, OPP_DN):
            return opp_r.at[kind - OPP_UP, lax.div(g, 2)]
        if kind in (DIR_UP, DIR_DN):
            return dir_r.at[kind - DIR_UP]
        return fwd_r.at[kind - FWD_UP, jnp.maximum(lax.div(g, 2), g - (groups - 1) + paired)]

    def piece(kind, g):
        src, dst, device = buffers[kind]
        return remote(src.at[g], dst.at[g], y_s.at[kind], landed(kind, g), device)

    def pieces(kind, g, n):
        src, dst, device = buffers[kind]
        some = pl.ds(g, n)
        return remote(src.at[some], dst.at[some], y_s.at[kind], landed(kind, g), device)

    sub = half // 3 if half % 3 == 0 and (half // 3) % LANES == 0 else half

    def coded(value, scale):
        return jnp.round(value * scale).astype(jnp.int32).astype(I16)

    def produce(g, sides):
        for side in sides:
            for at in range(0, half, sub):
                cols = slice(side * half + at, side * half + at + sub)
                into = slice(at, at + sub)
                part = dot(lhs, pair_v[g, :, cols])
                own[g, :, cols] = part[0:CHUNK]
                part = part[CHUNK:] - mid[CHUNK:]
                to_up, to_opp, to_dn = (part[i * CHUNK : (i + 1) * CHUNK] for i in range(3))
                i_up, i_opp, i_dn = (inv[i * CHUNK : (i + 1) * CHUNK] for i in range(1, Y))
                if side == 0:
                    opp_up_s[g, :, into] = coded(to_opp, i_opp)
                    hold_up[g, :, into] = to_up
                    dir_dn_s[g, :, into] = coded(to_dn, i_dn)
                else:
                    opp_dn_s[g, :, into] = coded(to_opp, i_opp)
                    hold_dn[g, :, into] = to_dn
                    dir_up_s[g, :, into] = coded(to_up, i_up)

    head_loads[0].wait()
    produce(0, (0,))

    pl.semaphore_wait(barrier, expected)
    piece(OPP_UP, 0).start()
    piece(DIR_DN, 0).start()
    head_loads[1].wait()
    produce(0, (1,))
    piece(OPP_DN, 0).start()
    piece(DIR_UP, 0).start()
    for k in range(1, Y):
        remote(weights.at[0], weights.at[Y - k], w_s, w_r, {"head": y_at(k)}).start()
    signal_all(near, waited)

    rounds = [d for d in (1, 2, 4) if d < zs]

    def tell(r):
        for present, other in (
            (z >= rounds[r], tok - rounds[r] * xs * CORES),
            (z < zs - rounds[r], tok + rounds[r] * xs * CORES),
        ):

            @pl.when(present)
            def _():
                signal(known.at[r], {"tok": other})

    def learn(r):
        amount = (z >= rounds[r]).astype(jnp.int32) + (z < zs - rounds[r]).astype(jnp.int32)
        pl.semaphore_wait(known.at[r], amount)

    loads[1].wait()
    loads[2].wait()
    single = single_v[...].astype(F32)
    normed = normalize(single).astype(BF16)
    query = (dot(normed, aqkv_v[0]) * (1.0 / math.sqrt(ATOM_HEAD_SIZE))).astype(BF16)
    kv_pad[RIM : RIM + atoms, 0:LANES] = dot(normed, aqkv_v[1]).astype(BF16)
    kv_pad[RIM : RIM + atoms, LANES:] = dot(normed, aqkv_v[2]).astype(BF16)
    halo_up = remote(
        kv_pad.at[pl.ds(atoms, RIM), :],
        kv_pad.at[pl.ds(0, RIM), :],
        halo_s.at[0],
        halo_r.at[0],
        {"tok": lax.rem(tok + 1, devs)},
    )
    halo_dn = remote(
        kv_pad.at[pl.ds(RIM, RIM), :],
        kv_pad.at[pl.ds(atoms + RIM, RIM), :],
        halo_s.at[1],
        halo_r.at[1],
        {"tok": lax.rem(tok + devs - 1, devs)},
    )

    def rest(g, carry):
        pair_load(g).wait()
        produce(g, (0, 1))
        for kind in (OPP_UP, OPP_DN, DIR_UP, DIR_DN):
            piece(kind, g).start()
        return carry

    lax.fori_loop(1, groups, rest, 0)

    @pl.when(back > 0)
    def _():
        pl.semaphore_wait(near, back)

    if len(rounds) > 0:
        tell(0)
    first, last = tok == 0, tok == devs - 1

    @pl.when(jnp.logical_not(last))
    def _():
        halo_up.start()

    @pl.when(jnp.logical_not(first))
    def _():
        halo_dn.start()

    def from_owner(value, k):
        shift = lax.rem((2 * Y - y - k) * columns, Y * columns)
        return pltpu.roll(value, shift, 1)[:, 0:LANES]

    for load in loads[4:]:
        load.wait()
    for i in range(4):
        proj_v[:, i * LANES : (i + 1) * LANES] = from_owner(
            qkvg_v[:, i, :].astype(F32), 0
        ).astype(BF16)
    for k in range(Y):
        out_v[:, k * LANES : (k + 1) * LANES] = from_owner(two_v[...].astype(F32), k).astype(BF16)
    if len(rounds) > 1:
        learn(0)
        tell(1)

    @pl.when(first)
    def _():
        kv_pad[0:RIM, :] = jnp.zeros((RIM, 2 * LANES), BF16)

    @pl.when(jnp.logical_not(first))
    def _():
        halo_up.wait_recv()
        halo_dn.wait_send()

    @pl.when(last)
    def _():
        kv_pad[atoms + RIM : atoms + 2 * RIM, :] = jnp.zeros((RIM, 2 * LANES), BF16)

    @pl.when(jnp.logical_not(last))
    def _():
        halo_dn.wait_recv()
        halo_up.wait_send()

    loads[3].wait()
    wide = WQ * ATOM_HEADS
    grow = mask(lax.div(iota((wide, WQ), 0), ATOM_HEADS) == iota((wide, WQ), 1)).astype(BF16)
    fold = mask(iota((WQ, wide), 0) == lax.div(iota((WQ, wide), 1), ATOM_HEADS)).astype(BF16)
    in_head = mask(
        lax.div(iota((wide, LANES), 1), ATOM_HEAD_SIZE) == lax.rem(iota((wide, LANES), 0), ATOM_HEADS)
    )
    slot = iota((wide, WK), 1)
    scores = []
    for w in range(windows):
        q_rows = (dot(grow, query[w * WQ : (w + 1) * WQ]) * in_head).astype(BF16)
        s = dot_nt(q_rows, kv_pad[w * WQ : w * WQ + WK, 0:LANES])
        s = s + bias_v[w * wide : (w + 1) * wide, :].astype(F32)
        if w * WQ < RIM or w * WQ + WK > RIM + atoms:
            spot = tok * atoms + w * WQ - RIM + slot
            s = jnp.where((spot >= 0) & (spot < devs * atoms), s, -1e30)
        scores.append(s)
    probs = []
    for s in scores:
        e = jnp.exp(s - jnp.max(s, axis=-1, keepdims=True))
        probs.append((e * (1.0 / jnp.sum(e, axis=-1, keepdims=True))).astype(BF16))
    mixes = []
    for w in range(windows):
        m = dot(probs[w], kv_pad[w * WQ : w * WQ + WK, LANES:])
        mixes.append(dot(fold, (m * in_head).astype(BF16)).astype(BF16))
    mix = jnp.concatenate(mixes, axis=0)
    a_out = (single + dot(mix, awo_v[...])).astype(BF16)
    atom_out[...] = a_out
    feat = jnp.maximum(dot(a_out, agg_v[...]), 0.0).astype(BF16)

    block = iota((BLOCK_DEVS * here, 1), 0)
    owner_tok = mate(lax.div(block, here)) * here + lax.rem(block, here)
    onehot = mask(owner_tok == name_v[...]).astype(BF16)
    sums = dot(onehot, feat)
    for k in range(1, BLOCK_DEVS):
        sum_s[k] = sums[k * here : (k + 1) * here].astype(BF16)
        remote(
            sum_s.at[k], sum_r.at[BLOCK_DEVS - k], sum_ss, sum_rs, {"tok": mate(k)}
        ).start()
    if len(rounds) > 2:
        learn(1)
        tell(2)

    others = pl.ds(1, BLOCK_DEVS - 1)
    remote(sum_s.at[others], sum_r.at[others], sum_ss, sum_rs, up).wait()
    total = sums[0:here]
    for k in range(1, BLOCK_DEVS):
        total = total + sum_r[k].astype(F32)
    square = iota((here, here), 0) == iota((here, here), 1)
    count = jnp.sum(jnp.where(square, count_v[...].astype(F32), 0.0), axis=1, keepdims=True)
    token_mid = tok_v[...].astype(F32) + total / count
    normed_t = normalize(token_mid).astype(BF16)
    parts = dot(normed_t, proj_v[...])
    t_query = (parts[:, 0:LANES] * (1.0 / math.sqrt(HEAD_SIZE))).astype(BF16)
    kv_all[z, x, c] = parts[:, LANES : 3 * LANES].astype(BF16)
    gate = jax.nn.sigmoid(parts[:, 3 * LANES :])
    residual = from_owner(token_mid, 0)

    if rounds:
        learn(len(rounds) - 1)
    sent = []
    for k in range(1, zs):
        block_k = kv_all.at[z, x, c]
        copy = remote(
            block_k, block_k, z_s.at[k], z_r.at[k], {"tok": tok_of(lax.rem(z + k, zs), x, c)}
        )
        copy.start()
        sent.append(copy)

    peers = pl.ds(1, Y - 1)
    remote(weights.at[peers], weights.at[peers], w_s, w_r, up).wait()
    r32 = iota((CHUNK, heads), 0)

    def reach_of(sender, k):
        head = y_at(k) * HL + lax.div(r32, ROWS)
        sel = mask(iota((CHUNK, heads), 1) == head).astype(BF16)
        chosen = dot(sel, weights[sender])
        return jnp.maximum(PAIR_HALF * jnp.sum(jnp.abs(chosen), axis=1, keepdims=True), 1e-20)

    step = 1.0 / CODE_MAX
    legs = []
    for kind, out, hold, src, k, to in (
        (OPP_UP, fwd_up_s, hold_up, opp_up_r, 1, FWD_UP),
        (OPP_DN, fwd_dn_s, hold_dn, opp_dn_r, 3, FWD_DN),
    ):
        theirs = reach_of(Y - k, k)
        legs.append((kind, out, hold, src, to, theirs * step, CODE_MAX / (theirs + reach_of(0, k))))
    r_up, r_opp, r_dn = (reach_of(k, 0) for k in range(1, Y))
    s_up, s_dn = r_up * step, r_dn * step
    s_up2, s_dn2 = (r_up + r_opp) * step, (r_dn + r_opp) * step

    def forward(pair_of, carry):
        for kind, out, hold, src, to, theirs, scale in legs:
            pieces(kind, 2 * pair_of, 2).wait_recv()
            for i in range(2):
                g = 2 * pair_of + i
                out[g] = coded(src[g].astype(F32) * theirs + hold[g], scale)
                piece(to, g).start()
        return carry

    lax.fori_loop(0, groups // 6, forward, 0)

    for k in range(1, zs):
        block_k = kv_all.at[lax.rem(z + zs - k, zs), x, c]
        remote(block_k, block_k, z_s.at[k], z_r.at[k], {"tok": tok}).wait_recv()

    def column(k):
        return kv_all.at[:, x_at(k), c]

    def send(ref, s_sem, r_sem, device):
        copy = remote(ref, ref, s_sem, r_sem, device)
        copy.start()
        return copy

    x_up, x_dn = {"tok": tok_of(z, x_at(1), c)}, {"tok": tok_of(z, x_at(xs - 1), c)}
    other = {"tok": tok_of(z, x, 1 - c)}
    sent.append(send(column(0), x_s.at[0], x_r.at[0], x_up))
    if xs > 2:
        sent.append(send(column(0), x_s.at[1], x_r.at[1], x_dn))
    send(column(0), c_s, c_r, other)

    lax.fori_loop(groups // 6, groups // 3, forward, 0)

    def arrived(ref, sem):
        remote(ref, ref, x_s.at[0], sem, other).wait_recv()

    arrived(column(xs - 1), x_r.at[0])
    if xs > 2:
        lower, upper = pl.ds(0, zs // 2), pl.ds(zs // 2, zs - zs // 2)
        sent.append(send(kv_all.at[lower, x_at(xs - 1), c], x_s.at[2], x_r.at[2], x_up))
        arrived(column(1), x_r.at[1])
        sent.append(send(kv_all.at[upper, x_at(1), c], x_s.at[3], x_r.at[2], x_dn))
        send(column(1), c_s, c_r, other)
    send(column(xs - 1), c_s, c_r, other)

    lax.fori_loop(groups // 3, groups // 2, forward, 0)

    if xs > 2:
        arrived(column(2), x_r.at[2])
        send(column(2), c_s, c_r, other)
    arrived(kv_all.at[:, :, 1 - c], c_r)

    rows = groups * CHUNK
    rr = iota((rows, here), 0)
    pick_row = lax.div(rr, CHUNK) * ROWS + lax.rem(rr, ROWS) == iota((rows, here), 1)
    rl = iota((rows, LANES), 0)
    of_head = mask(
        lax.div(iota((rows, LANES), 1), HEAD_SIZE) == lax.rem(lax.div(rl, ROWS), HL)
    )
    q_rows = (dot(mask(pick_row).astype(BF16), t_query) * of_head).astype(BF16)
    key_rows = kv_all[..., 0:LANES].reshape(keys, LANES)
    for at in range(0, keys, 2 * sub):
        s = dot_nt(q_rows, key_rows[at : at + 2 * sub])
        score[:, :, at : at + 2 * sub] = s.reshape(groups, CHUNK, 2 * sub)

    for kind in (DIR_UP, DIR_DN):
        pieces(kind, 0, groups).wait_recv()

    def direct(g, carry):
        for side, (ref, scale) in enumerate(((dir_dn_r, s_up), (dir_up_r, s_dn))):
            for at in range(0, half, sub):
                cols = slice(side * half + at, side * half + at + sub)
                got = ref[g, :, at : at + sub].astype(F32) * scale
                score[g, :, cols] = score[g, :, cols] + (own[g, :, cols] + got)
        return carry

    lax.fori_loop(0, groups, direct, 0)

    head_mask = of_head[0:CHUNK]

    def attend(g, carry):
        peak = None
        for side, (ref, scale) in enumerate(((fwd_up_r, s_dn2), (fwd_dn_r, s_up2))):
            for at in range(0, half, sub):
                cols = slice(side * half + at, side * half + at + sub)
                s = score[g, :, cols] + ref[g, :, at : at + sub].astype(F32) * scale
                score[g, :, cols] = s
                high = jnp.max(s, axis=-1, keepdims=True)
                peak = high if peak is None else jnp.maximum(peak, high)
        norm = jnp.zeros((CHUNK, 1), F32)
        acc = jnp.zeros((CHUNK, LANES), F32)
        value_rows = kv_all[..., LANES:].reshape(keys, LANES)
        for at in range(0, keys, sub):
            e = jnp.exp(score[g, :, at : at + sub] - peak)
            norm = norm + jnp.sum(e, axis=-1, keepdims=True)
            acc = acc + dot(e.astype(BF16), value_rows[at : at + sub])
        acc = acc * head_mask / norm
        mixed[g] = jnp.sum(acc.reshape(HL, ROWS, LANES), axis=0)
        return carry

    for g in range(0, groups - 2, 2):
        for kind in (FWD_UP, FWD_DN):
            pieces(kind, g, 2).wait_recv()
        lax.fori_loop(g, g + 2, attend, 0)
    for g in (groups - 2, groups - 1):
        for kind in (FWD_UP, FWD_DN):
            piece(kind, g).wait_recv()
        lax.fori_loop(g, g + 1, attend, 0)

    out_rows = (mixed[...].reshape(here, LANES) * gate).astype(BF16)
    term = dot(out_rows[:, 0:columns], out_v[...])
    for k in range(1, Y):
        fin_s[k] = term[:, k * LANES : (k + 1) * LANES].astype(BF16)
        remote(fin_s.at[k], fin_r.at[Y - k], fin_ss, fin_rs, {"head": y_at(k)}).start()
    for kind in range(6):
        pieces(kind, 0, groups).wait_send()
    for copy in sent:
        copy.wait_send()
    remote(kv_all.at[:, :, c], kv_all.at[:, :, c], c_s, c_r, other).wait_send()
    result = residual + term[:, 0:LANES]
    remote(fin_s.at[peers], fin_r.at[peers], fin_ss, fin_rs, up).wait()
    for k in range(1, Y):
        result = result + fin_r[k].astype(F32)
    token_out[...] = result[:, 0:columns].astype(BF16)


def per_device(
    atom_single,
    atom_bias,
    atom_token,
    atom_count,
    token_single,
    pair,
    atom_qkv,
    atom_wo,
    atom_agg,
    token_qkvg,
    pair_weight,
    token_wo,
):
    devs = lax.axis_size("tok")
    xs = 4 if devs % 32 == 0 else 2
    zs = devs // (xs * CORES)
    atoms, width = atom_single.shape
    here, width_t = token_single.shape
    keys = pair.shape[2]
    groups = here // ROWS
    half = keys // 2
    columns = width_t // Y
    depth = ROWS * CH
    anywhere = pl.BlockSpec(memory_space=pl.ANY)
    vmem = pl.BlockSpec(memory_space=pltpu.VMEM)
    dma = pltpu.SemaphoreType.DMA
    code = pltpu.VMEM((groups, CHUNK, half), I16)
    operands = (
        atom_single,
        atom_bias.reshape(atoms * ATOM_HEADS, WK),
        atom_token.reshape(1, atoms),
        atom_count.reshape(1, here),
        token_single,
        pair.reshape(here * CH, keys),
        jnp.transpose(atom_qkv, (1, 0, 2)),
        atom_wo,
        atom_agg,
        token_qkvg,
        jnp.transpose(pair_weight),
        token_wo,
    )
    scratch = [
        pltpu.VMEM((atoms, width), BF16),
        pltpu.VMEM((atoms * ATOM_HEADS, WK), BF16),
        pltpu.VMEM((1, atoms), jnp.int32),
        pltpu.VMEM((1, here), jnp.int32),
        pltpu.VMEM((here, width_t), BF16),
        pltpu.VMEM((groups, depth, keys), BF16),
        pltpu.VMEM((3, width, width), BF16),
        pltpu.VMEM(atom_wo.shape, BF16),
        pltpu.VMEM(atom_agg.shape, BF16),
        pltpu.VMEM(token_qkvg.shape, BF16),
        pltpu.VMEM(token_wo.shape, BF16),
        pltpu.VMEM((atoms + 2 * RIM, 2 * width), BF16),
        pltpu.VMEM((Y, Y * HL, CH), BF16),
        pltpu.VMEM((groups, CHUNK, keys), F32),
        pltpu.VMEM((groups, CHUNK, half), F32),
        pltpu.VMEM((groups, CHUNK, half), F32),
        *([code] * 12),
        pltpu.VMEM((BLOCK_DEVS, here, width_t), BF16),
        pltpu.VMEM((BLOCK_DEVS, here, width_t), BF16),
        pltpu.VMEM((zs, xs, CORES, here, 2 * LANES), BF16),
        pltpu.VMEM((groups, CHUNK, keys), F32),
        pltpu.VMEM((groups, ROWS, LANES), F32),
        pltpu.VMEM((Y, here, LANES), BF16),
        pltpu.VMEM((Y, here, LANES), BF16),
        pltpu.VMEM((width_t, 4 * LANES), BF16),
        pltpu.VMEM((columns, Y * LANES), BF16),
        dma((11,)),
        dma((groups + 1,)),
        dma((2,)),
        dma((2,)),
        dma,
        dma,
        dma((6,)),
        dma((2, groups // 2)),
        dma((2,)),
        dma((2, groups // 2 + 1)),
        dma,
        dma,
        dma((max(zs, 2),)),
        dma((max(zs, 2),)),
        dma((4,)),
        dma((3,)),
        dma,
        dma,
        dma,
        dma,
        pltpu.SemaphoreType.REGULAR((3,)),
        pltpu.SemaphoreType.REGULAR,
    ]
    outs = (
        pltpu.VMEM((atoms, width), BF16),
        pltpu.VMEM((here, columns), BF16),
    )
    return pl.pallas_call(
        functools.partial(fused, zs, xs),
        out_shape=outs,
        in_specs=[anywhere] * len(operands),
        out_specs=(vmem, vmem),
        scratch_shapes=scratch,
        compiler_params=pltpu.CompilerParams(
            collective_id=0, has_side_effects=True, vmem_limit_bytes=56 * 2**20
        ),
    )(*operands)


def solution(mesh):
    in_specs = (
        P("tok", None),
        P("tok", None, None),
        P("tok"),
        P("tok"),
        P("tok", None),
        P("tok", "head", None),
        P(),
        P(),
        P(),
        P(),
        P("head", None),
        P("head", None),
    )
    out_specs = (P("tok", None), P("tok", "head"))
    return jax.shard_map(
        per_device, mesh=mesh, in_specs=in_specs, out_specs=out_specs, check_vma=False
    )
```

profile of v0, /device:TPU:1, one launch (start us, length us, event | category | flops | bytes accessed | tf_op | source)
XLA Modules:
  0.0 49.2 jit_solution(4984678900280394622)
XLA Ops:
  0.6 47.3 %shard_map.131 = (bf16[480,128]{1,0:T(8,128)(2,1)S(1)}, bf16[48,96]{1,0:T(8,128)(2,1)S(1)}) custom-call(bf16[480,128]{1,0:T(8,128)(2,1)} %atom_single.1, bf16[1920,128]{1,0:T(8,128)(2,1)} %bitcast.7, s32[1,480]{1,0:T(1,128)} %bitcast.10, s32[1,48]{1,0:T(1,128)} %bitcast.11, bf16[48,384]{1,0:T(8,128)(2,1)} %token_single.1, bf16[1536,3072]{1,0:T(8,128)(2,1)} %bitcast.6, ...), custom_call_target="tpu_custom_call" | custom-call | tf_op jit(solution)/shard_map/pallas_call | solution.py:747
  47.9 0.7 %copy.16 = bf16[480,128]{1,0:T(8,128)(2,1)} copy(bf16[480,128]{1,0:T(8,128)(2,1)S(1)} %get-tuple-element.2) | data formatting | bytes 245760
  48.6 0.6 %copy.17 = bf16[48,96]{1,0:T(8,128)(2,1)} copy(bf16[48,96]{1,0:T(8,128)(2,1)S(1)} %get-tuple-element.3) | data formatting | bytes 18432
where the time goes:
time: 50.2 us; the launch traced here: 49.2 us
  Pallas kernels  47.3 us (94%)
  local copies, waits for them, and re-layouts  1.25 us (2%)
  between operations  0.64 us (1%)
    pallas_call x1, Pallas kernels, per_device(): pl.pallas_call(functools.partial(fused, zs, xs), out_shape=outs, in_specs...  47.3 us
    unnamed x2, local copies, waits for them, and re-layouts  1.25 us

commit v1 on v0

--- a/solution.py
+++ b/solution.py
@@ -136,6 +136,7 @@
     fin_rs,
     known,
     near,
+    opposite,
 ):
     tok = lax.axis_index("tok")
     y = lax.axis_index("head")
@@ -149,6 +150,7 @@
     here = tok_v.shape[0]
     atoms = single_v.shape[0]
     windows = atoms // WQ
+    sub = half // 3 if half % 3 == 0 else half
     columns = HL * HEAD_SIZE
     paired = groups // 2
 
@@ -180,8 +182,8 @@
         pl.semaphore_signal(sem, inc=1, device_id=device, device_id_type=MESH)
 
     barrier = pltpu.get_barrier_semaphore()
-    for k in range(1, Y):
-        signal(barrier, {"head": y_at(k)})
+    for device in (up, dn):
+        signal(barrier, device)
 
     loads = [
         (pair_weight, weights.at[0]),
@@ -207,11 +209,12 @@
 
     head_loads = [
         pltpu.make_async_copy(
-            pair.at[pl.ds(0, depth), pl.ds(side * half, half)],
-            pair_v.at[0, :, pl.ds(side * half, half)],
-            pair_sem.at[side * groups],
+            pair.at[pl.ds(0, depth), pl.ds(at, width)],
+            pair_v.at[0, :, pl.ds(at, width)],
+            pair_sem.at[sem],
         )
-        for side in range(2)
+        for at, width, sem in ((0, sub, 0), (sub, half - sub, groups), (half, half, groups + 1))
+        if width
     ]
     loads[0].start()
     for load in head_loads:
@@ -239,7 +242,7 @@
     def both(a, b):
         return b if a is None else a if b is True else jnp.logical_and(a, b)
 
-    waited, waiting, expected, back = [], [], Y - 1, 0
+    waited, waiting, expected, back = [], [], 2, 0
     for there, waits, other in edges:
         if waits is not False:
             waited.append((both(there, waits), other))
@@ -288,23 +291,29 @@
             return dir_r.at[kind - DIR_UP]
         return fwd_r.at[kind - FWD_UP, jnp.maximum(lax.div(g, 2), g - (groups - 1) + paired)]
 
+    def landed_last(kind, at):
+        return fwd_r.at[kind - FWD_UP, paired + (1 if at else 0)]
+
     def piece(kind, g):
         src, dst, device = buffers[kind]
         return remote(src.at[g], dst.at[g], y_s.at[kind], landed(kind, g), device)
+
+    def part_of(kind, g, at, width, sem):
+        src, dst, device = buffers[kind]
+        cols = pl.ds(at, width)
+        return remote(src.at[g, :, cols], dst.at[g, :, cols], y_s.at[kind], sem, device)
 
     def pieces(kind, g, n):
         src, dst, device = buffers[kind]
         some = pl.ds(g, n)
         return remote(src.at[some], dst.at[some], y_s.at[kind], landed(kind, g), device)
 
-    sub = half // 3 if half % 3 == 0 and (half // 3) % LANES == 0 else half
-
     def coded(value, scale):
         return jnp.round(value * scale).astype(jnp.int32).astype(I16)
 
-    def produce(g, sides):
+    def produce(g, sides, ats):
         for side in sides:
-            for at in range(0, half, sub):
+            for at in ats:
                 cols = slice(side * half + at, side * half + at + sub)
                 into = slice(at, at + sub)
                 part = dot(lhs, pair_v[g, :, cols])
@@ -321,18 +330,27 @@
                     hold_dn[g, :, into] = to_dn
                     dir_up_s[g, :, into] = coded(to_up, i_up)
 
+    ats = tuple(range(0, half, sub))
     head_loads[0].wait()
-    produce(0, (0,))
+    produce(0, (0,), ats[:1])
 
     pl.semaphore_wait(barrier, expected)
-    piece(OPP_UP, 0).start()
-    piece(DIR_DN, 0).start()
-    head_loads[1].wait()
-    produce(0, (1,))
-    piece(OPP_DN, 0).start()
-    piece(DIR_UP, 0).start()
-    for k in range(1, Y):
-        remote(weights.at[0], weights.at[Y - k], w_s, w_r, {"head": y_at(k)}).start()
+
+    def weights_copy(k):
+        to = {"head": y_at(k)}
+        return remote(weights.at[0], weights.at[Y - k], w_s, w_r.at[1 if k == 2 else 0], to)
+
+    weights_copy(1).start()
+    weights_copy(3).start()
+    for side in range(2):
+        for at in ats:
+            if side or at:
+                if at == ats[1 - side]:
+                    head_loads[1 + side].wait()
+                produce(0, (side,), (at,))
+            for kind in (OPP_DN, DIR_UP) if side else (OPP_UP, DIR_DN):
+                part_of(kind, 0, at, sub, landed(kind, 0)).start()
+    signal(opposite, up)
     signal_all(near, waited)
 
     rounds = [d for d in (1, 2, 4) if d < zs]
@@ -375,7 +393,7 @@
 
     def rest(g, carry):
         pair_load(g).wait()
-        produce(g, (0, 1))
+        produce(g, (0, 1), ats)
         for kind in (OPP_UP, OPP_DN, DIR_UP, DIR_DN):
             piece(kind, g).start()
         return carry
@@ -386,6 +404,8 @@
     def _():
         pl.semaphore_wait(near, back)
 
+    pl.semaphore_wait(opposite, 1)
+    weights_copy(2).start()
     if len(rounds) > 0:
         tell(0)
     first, last = tok == 0, tok == devs - 1
@@ -501,8 +521,8 @@
         copy.start()
         sent.append(copy)
 
-    peers = pl.ds(1, Y - 1)
-    remote(weights.at[peers], weights.at[peers], w_s, w_r, up).wait()
+    two = pl.ds(1, 2)
+    remote(weights.at[two], weights.at[two], w_s, w_r.at[0], up).wait_recv()
     r32 = iota((CHUNK, heads), 0)
 
     def reach_of(sender, k):
@@ -519,20 +539,29 @@
     ):
         theirs = reach_of(Y - k, k)
         legs.append((kind, out, hold, src, to, theirs * step, CODE_MAX / (theirs + reach_of(0, k))))
-    r_up, r_opp, r_dn = (reach_of(k, 0) for k in range(1, Y))
+    r_up, r_dn = reach_of(1, 0), reach_of(3, 0)
     s_up, s_dn = r_up * step, r_dn * step
-    s_up2, s_dn2 = (r_up + r_opp) * step, (r_dn + r_opp) * step
-
-    def forward(pair_of, carry):
+
+    early = half - sub if half > sub else half
+    last_parts = [(0, early), (early, half - early)] if early < half else [(0, half)]
+
+    def forward(g, last):
         for kind, out, hold, src, to, theirs, scale in legs:
-            pieces(kind, 2 * pair_of, 2).wait_recv()
-            for i in range(2):
-                g = 2 * pair_of + i
-                out[g] = coded(src[g].astype(F32) * theirs + hold[g], scale)
+            out[g] = coded(src[g].astype(F32) * theirs + hold[g], scale)
+            if not last:
                 piece(to, g).start()
-        return carry
-
-    lax.fori_loop(0, groups // 6, forward, 0)
+        if last:
+            for at, width in last_parts:
+                for to in (FWD_UP, FWD_DN):
+                    part_of(to, g, at, width, landed_last(to, at)).start()
+
+    def forward_two(i, last=False):
+        for kind in (OPP_UP, OPP_DN):
+            pieces(kind, 2 * i, 2).wait_recv()
+        forward(2 * i, False)
+        forward(2 * i + 1, last)
+
+    forward_two(0)
 
     for k in range(1, zs):
         block_k = kv_all.at[lax.rem(z + zs - k, zs), x, c]
@@ -553,7 +582,7 @@
         sent.append(send(column(0), x_s.at[1], x_r.at[1], x_dn))
     send(column(0), c_s, c_r, other)
 
-    lax.fori_loop(groups // 6, groups // 3, forward, 0)
+    forward_two(1)
 
     def arrived(ref, sem):
         remote(ref, ref, x_s.at[0], sem, other).wait_recv()
@@ -567,7 +596,7 @@
         send(column(1), c_s, c_r, other)
     send(column(xs - 1), c_s, c_r, other)
 
-    lax.fori_loop(groups // 3, groups // 2, forward, 0)
+    forward_two(2, True)
 
     if xs > 2:
         arrived(column(2), x_r.at[2])
@@ -602,42 +631,64 @@
 
     head_mask = of_head[0:CHUNK]
 
-    def attend(g, carry):
-        peak = None
+    weights_copy(2).wait_recv()
+    r_opp = reach_of(2, 0)
+    s_up2, s_dn2 = (r_up + r_opp) * step, (r_dn + r_opp) * step
+
+    def attend_part(g, at_first, width, state):
+        spans = []
+        peak = state[0] if state else None
         for side, (ref, scale) in enumerate(((fwd_up_r, s_dn2), (fwd_dn_r, s_up2))):
-            for at in range(0, half, sub):
+            for at in range(at_first, at_first + width, sub):
                 cols = slice(side * half + at, side * half + at + sub)
                 s = score[g, :, cols] + ref[g, :, at : at + sub].astype(F32) * scale
                 score[g, :, cols] = s
+                spans.append(cols)
                 high = jnp.max(s, axis=-1, keepdims=True)
                 peak = high if peak is None else jnp.maximum(peak, high)
-        norm = jnp.zeros((CHUNK, 1), F32)
-        acc = jnp.zeros((CHUNK, LANES), F32)
+        if state:
+            shrink = jnp.exp(state[0] - peak)
+            norm, acc = state[1] * shrink, state[2] * shrink
+        else:
+            norm, acc = jnp.zeros((CHUNK, 1), F32), jnp.zeros((CHUNK, LANES), F32)
         value_rows = kv_all[..., LANES:].reshape(keys, LANES)
-        for at in range(0, keys, sub):
-            e = jnp.exp(score[g, :, at : at + sub] - peak)
+        for cols in spans:
+            e = jnp.exp(score[g, :, cols] - peak)
             norm = norm + jnp.sum(e, axis=-1, keepdims=True)
-            acc = acc + dot(e.astype(BF16), value_rows[at : at + sub])
-        acc = acc * head_mask / norm
+            acc = acc + dot(e.astype(BF16), value_rows[cols])
+        return peak, norm, acc
+
+    def finish(g, state):
+        acc = state[2] * head_mask / state[1]
         mixed[g] = jnp.sum(acc.reshape(HL, ROWS, LANES), axis=0)
+
+    def attend(g, carry):
+        finish(g, attend_part(g, 0, half, None))
         return carry
 
     for g in range(0, groups - 2, 2):
         for kind in (FWD_UP, FWD_DN):
             pieces(kind, g, 2).wait_recv()
         lax.fori_loop(g, g + 2, attend, 0)
-    for g in (groups - 2, groups - 1):
+    for kind in (FWD_UP, FWD_DN):
+        piece(kind, groups - 2).wait_recv()
+    attend(groups - 2, 0)
+    state = None
+    for at, width in last_parts:
         for kind in (FWD_UP, FWD_DN):
-            piece(kind, g).wait_recv()
-        lax.fori_loop(g, g + 1, attend, 0)
+            part_of(kind, groups - 1, at, width, landed_last(kind, at)).wait_recv()
+        state = attend_part(groups - 1, at, width, state)
+    finish(groups - 1, state)
 
     out_rows = (mixed[...].reshape(here, LANES) * gate).astype(BF16)
     term = dot(out_rows[:, 0:columns], out_v[...])
     for k in range(1, Y):
         fin_s[k] = term[:, k * LANES : (k + 1) * LANES].astype(BF16)
         remote(fin_s.at[k], fin_r.at[Y - k], fin_ss, fin_rs, {"head": y_at(k)}).start()
+    peers = pl.ds(1, Y - 1)
     for kind in range(6):
         pieces(kind, 0, groups).wait_send()
+    remote(weights.at[peers], weights.at[peers], w_s, w_r.at[0], up).wait_send()
     for copy in sent:
         copy.wait_send()
     remote(kv_all.at[:, :, c], kv_all.at[:, :, c], c_s, c_r, other).wait_send()
@@ -646,6 +697,17 @@
     for k in range(1, Y):
         result = result + fin_r[k].astype(F32)
     token_out[...] = result[:, 0:columns].astype(BF16)
+
+
+def hand_over(a, b, a_out, b_out, sems):
+    copies = [
+        pltpu.make_async_copy(a, a_out, sems.at[0]),
+        pltpu.make_async_copy(b, b_out, sems.at[1]),
+    ]
+    for copy in copies:
+        copy.start()
+    for copy in copies:
+        copy.wait()
 
 
 def per_device(
@@ -718,15 +780,15 @@
         pltpu.VMEM((width_t, 4 * LANES), BF16),
         pltpu.VMEM((columns, Y * LANES), BF16),
         dma((11,)),
-        dma((groups + 1,)),
+        dma((groups + 2,)),
         dma((2,)),
         dma((2,)),
         dma,
-        dma,
+        dma((2,)),
         dma((6,)),
         dma((2, groups // 2)),
         dma((2,)),
-        dma((2, groups // 2 + 1)),
+        dma((2, groups // 2 + 2)),
         dma,
         dma,
         dma((max(zs, 2),)),
@@ -739,12 +801,13 @@
         dma,
         pltpu.SemaphoreType.REGULAR((3,)),
         pltpu.SemaphoreType.REGULAR,
+        pltpu.SemaphoreType.REGULAR,
     ]
     outs = (
         pltpu.VMEM((atoms, width), BF16),
         pltpu.VMEM((here, columns), BF16),
     )
-    return pl.pallas_call(
+    results = pl.pallas_call(
         functools.partial(fused, zs, xs),
         out_shape=outs,
         in_specs=[anywhere] * len(operands),
@@ -754,6 +817,14 @@
             collective_id=0, has_side_effects=True, vmem_limit_bytes=56 * 2**20
         ),
     )(*operands)
+    results = [pltpu.with_memory_space_constraint(r, pltpu.VMEM) for r in results]
+    return pl.pallas_call(
+        hand_over,
+        out_shape=tuple(pltpu.HBM(r.shape, r.dtype) for r in results),
+        in_specs=[anywhere, anywhere],
+        out_specs=(anywhere, anywhere),
+        scratch_shapes=[dma((2,))],
+    )(*results)
 
 
 def solution(mesh):

time: 50.2 us -> 49.6 us (0.988); the launches traced: 49.2 us -> 49.2 us
  Pallas kernels: 47.3 us -> 48.6 us
  local copies, waits for them, and re-layouts: 1.25 us -> 0 us
    unnamed x2 -> x0, local copies, waits for them, and re-layouts: 1.25 us -> none
    pallas_call x0 -> x1, Pallas kernels: none -> 0.67 us  [per_device(): pl.pallas_call(hand_over, out_shape=tuple((pltpu.HBM(r.shape, r.dtype) fo...]
    pallas_call x1, Pallas kernels: 47.3 us -> 47.9 us  [per_device(): pl.pallas_call(functools.partial(fused, zs, xs), out_shape=outs, in_specs...]
where the time goes in v1:
time: 49.6 us; the launch traced here: 49.2 us
  Pallas kernels  48.6 us (98%)
  between operations  0.64 us (1%)
    pallas_call x1, Pallas kernels, per_device(): pl.pallas_call(functools.partial(fused, zs, xs), out_shape=outs, in_specs...  47.9 us

profile of v1, /device:TPU:1, one launch (start us, length us, event | category | flops | bytes accessed | tf_op | source)
XLA Modules:
  0.0 49.2 jit_solution(4011134592238578530)
XLA Ops:
  0.6 47.9 %shard_map.131 = (bf16[480,128]{1,0:T(8,128)(2,1)S(1)}, bf16[48,96]{1,0:T(8,128)(2,1)S(1)}) custom-call(bf16[480,128]{1,0:T(8,128)(2,1)} %atom_single.1, bf16[1920,128]{1,0:T(8,128)(2,1)} %bitcast.7, s32[1,480]{1,0:T(1,128)} %bitcast.10, s32[1,48]{1,0:T(1,128)} %bitcast.11, bf16[48,384]{1,0:T(8,128)(2,1)} %token_single.1, bf16[1536,3072]{1,0:T(8,128)(2,1)} %bitcast.6, ...), custom_call_target="tpu_custom_call" | custom-call | tf_op jit(solution)/shard_map/pallas_call | solution.py:810
  48.5 0.7 %shard_map.132 = (bf16[480,128]{1,0:T(8,128)(2,1)}, bf16[48,96]{1,0:T(8,128)(2,1)}) custom-call(bf16[480,128]{1,0:T(8,128)(2,1)S(1)} %get-tuple-element.4.a, bf16[48,96]{1,0:T(8,128)(2,1)S(1)} %get-tuple-element.5.b), custom_call_target="tpu_custom_call" | custom-call | tf_op jit(solution)/shard_map/pallas_call | solution.py:821

commit v2 on v1

--- a/solution.py
+++ b/solution.py
@@ -93,12 +93,7 @@
     own,
     hold_up,
     hold_dn,
-    opp_up_s,
-    opp_dn_s,
-    dir_up_s,
-    dir_dn_s,
-    fwd_up_s,
-    fwd_dn_s,
+    codes_s,
     opp_up_r,
     opp_dn_r,
     dir_up_r,
@@ -185,6 +180,8 @@
     for device in (up, dn):
         signal(barrier, device)
 
+    opp_up_s, opp_dn_s, dir_up_s, dir_dn_s, fwd_up_s, fwd_dn_s = (codes_s.at[i] for i in range(6))
+
     loads = [
         (pair_weight, weights.at[0]),
         (atom_single, single_v),
@@ -204,7 +201,7 @@
         return pltpu.make_async_copy(
             pair.at[pl.ds(pl.multiple_of(g * depth, depth), depth), :],
             pair_v.at[g],
-            pair_sem.at[g],
+            pair_sem.at[5 if g == 1 else g // 2],
         )
 
     head_loads = [
@@ -213,7 +210,7 @@
             pair_v.at[0, :, pl.ds(at, width)],
             pair_sem.at[sem],
         )
-        for at, width, sem in ((0, sub, 0), (sub, half - sub, groups), (half, half, groups + 1))
+        for at, width, sem in ((0, sub, 0), (sub, half - sub, 3), (half, half, 4))
         if width
     ]
     loads[0].start()
@@ -296,17 +293,17 @@
 
     def piece(kind, g):
         src, dst, device = buffers[kind]
-        return remote(src.at[g], dst.at[g], y_s.at[kind], landed(kind, g), device)
+        return remote(src.at[g], dst.at[g], y_s, landed(kind, g), device)
 
     def part_of(kind, g, at, width, sem):
         src, dst, device = buffers[kind]
         cols = pl.ds(at, width)
-        return remote(src.at[g, :, cols], dst.at[g, :, cols], y_s.at[kind], sem, device)
+        return remote(src.at[g, :, cols], dst.at[g, :, cols], y_s, sem, device)
 
     def pieces(kind, g, n):
         src, dst, device = buffers[kind]
         some = pl.ds(g, n)
-        return remote(src.at[some], dst.at[some], y_s.at[kind], landed(kind, g), device)
+        return remote(src.at[some], dst.at[some], y_s, landed(kind, g), device)
 
     def coded(value, scale):
         return jnp.round(value * scale).astype(jnp.int32).astype(I16)
@@ -340,8 +337,6 @@
         to = {"head": y_at(k)}
         return remote(weights.at[0], weights.at[Y - k], w_s, w_r.at[1 if k == 2 else 0], to)
 
-    weights_copy(1).start()
-    weights_copy(3).start()
     for side in range(2):
         for at in ats:
             if side or at:
@@ -350,6 +345,8 @@
                 produce(0, (side,), (at,))
             for kind in (OPP_DN, DIR_UP) if side else (OPP_UP, DIR_DN):
                 part_of(kind, 0, at, sub, landed(kind, 0)).start()
+    weights_copy(1).start()
+    weights_copy(3).start()
     signal(opposite, up)
     signal_all(near, waited)
 
@@ -392,13 +389,17 @@
     )
 
     def rest(g, carry):
-        pair_load(g).wait()
         produce(g, (0, 1), ats)
         for kind in (OPP_UP, OPP_DN, DIR_UP, DIR_DN):
             piece(kind, g).start()
         return carry
 
-    lax.fori_loop(1, groups, rest, 0)
+    pair_load(1).wait()
+    rest(1, 0)
+    for g in range(2, groups, 2):
+        two_groups = pair_v.at[pl.ds(g, 2)]
+        pltpu.make_async_copy(two_groups, two_groups, pair_sem.at[g // 2]).wait()
+        lax.fori_loop(g, g + 2, rest, 0)
 
     @pl.when(back > 0)
     def _():
@@ -512,14 +513,9 @@
 
     if rounds:
         learn(len(rounds) - 1)
-    sent = []
     for k in range(1, zs):
         block_k = kv_all.at[z, x, c]
-        copy = remote(
-            block_k, block_k, z_s.at[k], z_r.at[k], {"tok": tok_of(lax.rem(z + k, zs), x, c)}
-        )
-        copy.start()
-        sent.append(copy)
+        remote(block_k, block_k, z_s, z_r, {"tok": tok_of(lax.rem(z + k, zs), x, c)}).start()
 
     two = pl.ds(1, 2)
     remote(weights.at[two], weights.at[two], w_s, w_r.at[0], up).wait_recv()
@@ -563,9 +559,9 @@
 
     forward_two(0)
 
-    for k in range(1, zs):
-        block_k = kv_all.at[lax.rem(z + zs - k, zs), x, c]
-        remote(block_k, block_k, z_s.at[k], z_r.at[k], {"tok": tok}).wait_recv()
+    if zs > 1:
+        others_z = kv_all.at[pl.ds(0, zs - 1), x, c]
+        remote(others_z, others_z, z_s, z_r, {"tok": tok}).wait_recv()
 
     def column(k):
         return kv_all.at[:, x_at(k), c]
@@ -577,22 +573,22 @@
 
     x_up, x_dn = {"tok": tok_of(z, x_at(1), c)}, {"tok": tok_of(z, x_at(xs - 1), c)}
     other = {"tok": tok_of(z, x, 1 - c)}
-    sent.append(send(column(0), x_s.at[0], x_r.at[0], x_up))
+    send(column(0), x_s, x_r.at[0], x_up)
     if xs > 2:
-        sent.append(send(column(0), x_s.at[1], x_r.at[1], x_dn))
+        send(column(0), x_s, x_r.at[1], x_dn)
     send(column(0), c_s, c_r, other)
 
     forward_two(1)
 
     def arrived(ref, sem):
-        remote(ref, ref, x_s.at[0], sem, other).wait_recv()
+        remote(ref, ref, x_s, sem, other).wait_recv()
 
     arrived(column(xs - 1), x_r.at[0])
     if xs > 2:
         lower, upper = pl.ds(0, zs // 2), pl.ds(zs // 2, zs - zs // 2)
-        sent.append(send(kv_all.at[lower, x_at(xs - 1), c], x_s.at[2], x_r.at[2], x_up))
+        send(kv_all.at[lower, x_at(xs - 1), c], x_s, x_r.at[2], x_up)
         arrived(column(1), x_r.at[1])
-        sent.append(send(kv_all.at[upper, x_at(1), c], x_s.at[3], x_r.at[2], x_dn))
+        send(kv_all.at[upper, x_at(1), c], x_s, x_r.at[2], x_dn)
         send(column(1), c_s, c_r, other)
     send(column(xs - 1), c_s, c_r, other)
 
@@ -684,13 +680,17 @@
     term = dot(out_rows[:, 0:columns], out_v[...])
     for k in range(1, Y):
         fin_s[k] = term[:, k * LANES : (k + 1) * LANES].astype(BF16)
-        remote(fin_s.at[k], fin_r.at[Y - k], fin_ss, fin_rs, {"head": y_at(k)}).start()
+    for i in range(Y - 1):
+        target = i + (y <= i).astype(jnp.int32)
+        k = lax.rem(target - y + Y, Y)
+        remote(fin_s.at[k], fin_r.at[Y - k], fin_ss, fin_rs, {"head": target}).start()
     peers = pl.ds(1, Y - 1)
-    for kind in range(6):
-        pieces(kind, 0, groups).wait_send()
+    remote(codes_s, codes_s, y_s, w_r.at[0], up).wait_send()
     remote(weights.at[peers], weights.at[peers], w_s, w_r.at[0], up).wait_send()
-    for copy in sent:
-        copy.wait_send()
+    if zs > 1:
+        remote(others_z, others_z, z_s, z_r, other).wait_send()
+    x_sent = kv_all.at[:, pl.ds(0, 3 if xs > 2 else 1), c]
+    remote(x_sent, x_sent, x_s, x_r.at[0], other).wait_send()
     remote(kv_all.at[:, :, c], kv_all.at[:, :, c], c_s, c_r, other).wait_send()
     result = residual + term[:, 0:LANES]
     remote(fin_s.at[peers], fin_r.at[peers], fin_ss, fin_rs, up).wait()
@@ -769,7 +769,8 @@
         pltpu.VMEM((groups, CHUNK, keys), F32),
         pltpu.VMEM((groups, CHUNK, half), F32),
         pltpu.VMEM((groups, CHUNK, half), F32),
-        *([code] * 12),
+        pltpu.VMEM((6, groups, CHUNK, half), I16),
+        *([code] * 6),
         pltpu.VMEM((BLOCK_DEVS, here, width_t), BF16),
         pltpu.VMEM((BLOCK_DEVS, here, width_t), BF16),
         pltpu.VMEM((zs, xs, CORES, here, 2 * LANES), BF16),
@@ -780,20 +781,20 @@
         pltpu.VMEM((width_t, 4 * LANES), BF16),
         pltpu.VMEM((columns, Y * LANES), BF16),
         dma((11,)),
-        dma((groups + 2,)),
+        dma((6,)),
         dma((2,)),
         dma((2,)),
         dma,
         dma((2,)),
-        dma((6,)),
+        dma,
         dma((2, groups // 2)),
         dma((2,)),
         dma((2, groups // 2 + 2)),
         dma,
         dma,
-        dma((max(zs, 2),)),
-        dma((max(zs, 2),)),
-        dma((4,)),
+        dma,
+        dma,
+        dma,
         dma((3,)),
         dma,
         dma,

time: 49.6 us -> 49.3 us (level)
  no operation moved by 1% of the time
where the time goes in v2:
time: 49.3 us; the launch traced here: 49 us
  Pallas kernels  48.3 us (98%)
  between operations  0.64 us (1%)
    pallas_call x1, Pallas kernels, per_device(): pl.pallas_call(functools.partial(fused, zs, xs), out_shape=outs, in_specs...  47.7 us

profile of v2, /device:TPU:1, one launch (start us, length us, event | category | flops | bytes accessed | tf_op | source)
XLA Modules:
  0.0 49.0 jit_solution(16837738585459476880)
XLA Ops:
  0.6 47.7 %shard_map.131 = (bf16[480,128]{1,0:T(8,128)(2,1)S(1)}, bf16[48,96]{1,0:T(8,128)(2,1)S(1)}) custom-call(bf16[480,128]{1,0:T(8,128)(2,1)} %atom_single.1, bf16[1920,128]{1,0:T(8,128)(2,1)} %bitcast.7, s32[1,480]{1,0:T(1,128)} %bitcast.10, s32[1,48]{1,0:T(1,128)} %bitcast.11, bf16[48,384]{1,0:T(8,128)(2,1)} %token_single.1, bf16[1536,3072]{1,0:T(8,128)(2,1)} %bitcast.6, ...), custom_call_target="tpu_custom_call" | custom-call | tf_op jit(solution)/shard_map/pallas_call | solution.py:811
  48.3 0.7 %shard_map.132 = (bf16[480,128]{1,0:T(8,128)(2,1)}, bf16[48,96]{1,0:T(8,128)(2,1)}) custom-call(bf16[480,128]{1,0:T(8,128)(2,1)S(1)} %get-tuple-element.4.a, bf16[48,96]{1,0:T(8,128)(2,1)S(1)} %get-tuple-element.5.b), custom_call_target="tpu_custom_call" | custom-call | tf_op jit(solution)/shard_map/pallas_call | solution.py:822

commit v3 on v2

--- a/solution.py
+++ b/solution.py
@@ -218,10 +218,6 @@
         load.start()
     loads[1].start()
     loads[2].start()
-    for g in range(1, groups):
-        pair_load(g).start()
-    for load in loads[3:]:
-        load.start()
 
     first_core = c == 0
     edges = []
@@ -257,17 +253,18 @@
 
     signal_all(barrier, waiting)
 
-    loads[0].wait()
-    wt = weights[0]
-    heads = wt.shape[0]
+    heads = weights.shape[1]
     row = iota((Y * CHUNK, heads), 0)
     owner = lax.rem(y + lax.div(row, CHUNK), Y)
     pick = iota((Y * CHUNK, heads), 1) == owner * HL + lax.rem(lax.div(row, ROWS), HL)
-    picked = dot(mask(pick).astype(BF16), wt).astype(BF16)
-    spread = mask(iota((CH, depth), 0) == lax.rem(iota((CH, depth), 1), CH)).astype(BF16)
+    pick = mask(pick).astype(BF16)
     diag = lax.div(iota((Y * CHUNK, depth), 1), CH) == lax.rem(iota((Y * CHUNK, depth), 0), ROWS)
-    lhs = (dot(picked, spread) * mask(diag)).astype(BF16)
-    picked_f = picked.astype(F32)
+    diag = mask(diag)
+    loads[0].wait()
+    tiled = jnp.concatenate([weights[0]] * ROWS, axis=1)
+    picked_f = dot(pick, tiled)
+    lhs = (picked_f * diag).astype(BF16)
+    picked_f = picked_f[:, 0:CH]
     mid = PAIR_MID * jnp.sum(picked_f, axis=1, keepdims=True)
     reach = jnp.maximum(PAIR_HALF * jnp.sum(jnp.abs(picked_f), axis=1, keepdims=True), 1e-20)
     inv = CODE_MAX / reach
@@ -329,6 +326,10 @@
 
     ats = tuple(range(0, half, sub))
     head_loads[0].wait()
+    for g in range(1, groups):
+        pair_load(g).start()
+    for load in loads[3:]:
+        load.start()
     produce(0, (0,), ats[:1])
 
     pl.semaphore_wait(barrier, expected)
@@ -662,10 +663,43 @@
         finish(g, attend_part(g, 0, half, None))
         return carry
 
+    cut = (groups - 2) * ROWS
+    out_parts = [(0, cut), (cut, here - cut)]
+
+    def hand_out(i):
+        at, n = out_parts[i]
+        mix_rows = mixed[at // ROWS : (at + n) // ROWS].reshape(n, LANES)
+        out_rows = (mix_rows * gate[at : at + n]).astype(BF16)
+        term = dot(out_rows[:, 0:columns], out_v[...])
+        for k in range(1, Y):
+            fin_s[k, at : at + n] = term[:, k * LANES : (k + 1) * LANES].astype(BF16)
+        for j in range(Y - 1):
+            target = j + (y <= j).astype(jnp.int32)
+            k = lax.rem(target - y + Y, Y)
+            some = pl.ds(at, n)
+            remote(
+                fin_s.at[k, some],
+                fin_r.at[Y - k, some],
+                fin_ss.at[i],
+                fin_rs.at[i],
+                {"head": target},
+            ).start()
+        return residual[at : at + n] + term[:, 0:LANES]
+
+    def take_in(i, result):
+        at, n = out_parts[i]
+        part = fin_r.at[pl.ds(1, Y - 1), pl.ds(at, n)]
+        sent = fin_s.at[pl.ds(1, Y - 1), pl.ds(at, n)]
+        remote(sent, part, fin_ss.at[i], fin_rs.at[i], up).wait()
+        for k in range(1, Y):
+            result = result + fin_r[k, at : at + n].astype(F32)
+        token_out[at : at + n] = result[:, 0:columns].astype(BF16)
+
     for g in range(0, groups - 2, 2):
         for kind in (FWD_UP, FWD_DN):
             pieces(kind, g, 2).wait_recv()
         lax.fori_loop(g, g + 2, attend, 0)
+    early_rows = hand_out(0)
     for kind in (FWD_UP, FWD_DN):
         piece(kind, groups - 2).wait_recv()
     attend(groups - 2, 0)
@@ -676,14 +710,7 @@
         state = attend_part(groups - 1, at, width, state)
     finish(groups - 1, state)
 
-    out_rows = (mixed[...].reshape(here, LANES) * gate).astype(BF16)
-    term = dot(out_rows[:, 0:columns], out_v[...])
-    for k in range(1, Y):
-        fin_s[k] = term[:, k * LANES : (k + 1) * LANES].astype(BF16)
-    for i in range(Y - 1):
-        target = i + (y <= i).astype(jnp.int32)
-        k = lax.rem(target - y + Y, Y)
-        remote(fin_s.at[k], fin_r.at[Y - k], fin_ss, fin_rs, {"head": target}).start()
+    late_rows = hand_out(1)
     peers = pl.ds(1, Y - 1)
     remote(codes_s, codes_s, y_s, w_r.at[0], up).wait_send()
     remote(weights.at[peers], weights.at[peers], w_s, w_r.at[0], up).wait_send()
@@ -692,11 +719,8 @@
     x_sent = kv_all.at[:, pl.ds(0, 3 if xs > 2 else 1), c]
     remote(x_sent, x_sent, x_s, x_r.at[0], other).wait_send()
     remote(kv_all.at[:, :, c], kv_all.at[:, :, c], c_s, c_r, other).wait_send()
-    result = residual + term[:, 0:LANES]
-    remote(fin_s.at[peers], fin_r.at[peers], fin_ss, fin_rs, up).wait()
-    for k in range(1, Y):
-        result = result + fin_r[k].astype(F32)
-    token_out[...] = result[:, 0:columns].astype(BF16)
+    take_in(0, early_rows)
+    take_in(1, late_rows)
 
 
 def hand_over(a, b, a_out, b_out, sems):
@@ -798,8 +822,8 @@
         dma((3,)),
         dma,
         dma,
-        dma,
-        dma,
+        dma((2,)),
+        dma((2,)),
         pltpu.SemaphoreType.REGULAR((3,)),
         pltpu.SemaphoreType.REGULAR,
         pltpu.SemaphoreType.REGULAR,

time: 49.3 us -> 49.2 us (level)
  no operation moved by 1% of the time
where the time goes in v3:
time: 49.2 us; the launch traced here: 49.1 us
  Pallas kernels  48.5 us (99%)
  between operations  0.64 us (1%)
    pallas_call x1, Pallas kernels, per_device(): pl.pallas_call(functools.partial(fused, zs, xs), out_shape=outs, in_specs...  47.8 us

profile of v3, /device:TPU:1, one launch (start us, length us, event | category | flops | bytes accessed | tf_op | source)
XLA Modules:
  0.0 49.1 jit_solution(13766044668326058829)
XLA Ops:
  0.6 47.8 %shard_map.131 = (bf16[480,128]{1,0:T(8,128)(2,1)S(1)}, bf16[48,96]{1,0:T(8,128)(2,1)S(1)}) custom-call(bf16[480,128]{1,0:T(8,128)(2,1)} %atom_single.1, bf16[1920,128]{1,0:T(8,128)(2,1)} %bitcast.7, s32[1,480]{1,0:T(1,128)} %bitcast.10, s32[1,48]{1,0:T(1,128)} %bitcast.11, bf16[48,384]{1,0:T(8,128)(2,1)} %token_single.1, bf16[1536,3072]{1,0:T(8,128)(2,1)} %bitcast.6, ...), custom_call_target="tpu_custom_call" | custom-call | tf_op jit(solution)/shard_map/pallas_call | solution.py:835
  48.5 0.7 %shard_map.132 = (bf16[480,128]{1,0:T(8,128)(2,1)}, bf16[48,96]{1,0:T(8,128)(2,1)}) custom-call(bf16[480,128]{1,0:T(8,128)(2,1)S(1)} %get-tuple-element.4.a, bf16[48,96]{1,0:T(8,128)(2,1)S(1)} %get-tuple-element.5.b), custom_call_target="tpu_custom_call" | custom-call | tf_op jit(solution)/shard_map/pallas_call | solution.py:846

commit v4 on v3

--- a/solution.py
+++ b/solution.py
@@ -218,6 +218,10 @@
         load.start()
     loads[1].start()
     loads[2].start()
+    for g in range(1, groups):
+        pair_load(g).start()
+    for load in loads[3:]:
+        load.start()
 
     first_core = c == 0
     edges = []
@@ -326,10 +330,6 @@
 
     ats = tuple(range(0, half, sub))
     head_loads[0].wait()
-    for g in range(1, groups):
-        pair_load(g).start()
-    for load in loads[3:]:
-        load.start()
     produce(0, (0,), ats[:1])
 
     pl.semaphore_wait(barrier, expected)

time: 49.2 us -> 49.2 us (level)
  no operation moved by 1% of the time
where the time goes in v4:
time: 49.2 us; the launch traced here: 49.1 us
  Pallas kernels  48.4 us (98%)
  between operations  0.64 us (1%)
    pallas_call x1, Pallas kernels, per_device(): pl.pallas_call(functools.partial(fused, zs, xs), out_shape=outs, in_specs...  47.7 us

profile of v4, /device:TPU:1, one launch (start us, length us, event | category | flops | bytes accessed | tf_op | source)
XLA Modules:
  0.0 49.1 jit_solution(12548777051720211923)
XLA Ops:
  0.6 47.7 %shard_map.131 = (bf16[480,128]{1,0:T(8,128)(2,1)S(1)}, bf16[48,96]{1,0:T(8,128)(2,1)S(1)}) custom-call(bf16[480,128]{1,0:T(8,128)(2,1)} %atom_single.1, bf16[1920,128]{1,0:T(8,128)(2,1)} %bitcast.7, s32[1,480]{1,0:T(1,128)} %bitcast.10, s32[1,48]{1,0:T(1,128)} %bitcast.11, bf16[48,384]{1,0:T(8,128)(2,1)} %token_single.1, bf16[1536,3072]{1,0:T(8,128)(2,1)} %bitcast.6, ...), custom_call_target="tpu_custom_call" | custom-call | tf_op jit(solution)/shard_map/pallas_call | solution.py:835
  48.4 0.7 %shard_map.132 = (bf16[480,128]{1,0:T(8,128)(2,1)}, bf16[48,96]{1,0:T(8,128)(2,1)}) custom-call(bf16[480,128]{1,0:T(8,128)(2,1)S(1)} %get-tuple-element.4.a, bf16[48,96]{1,0:T(8,128)(2,1)S(1)} %get-tuple-element.5.b), custom_call_target="tpu_custom_call" | custom-call | tf_op jit(solution)/shard_map/pallas_call | solution.py:846
